TPU v7x, 32 devices: a whole 2x2x4 slice. The times are simulated.
32 devices in a mesh: dp: 16 (over z, y, core), book: 2 (over x).
Axes of the slice: x: 2, y: 2, z: 4, core: 2. Of those that a mesh axis runs over, the one named last changes fastest.
Arguments:
- corpus_rows: bfloat16 [12288, 1024], P('dp'), may hold values from -6 to 6
- code_ids: int32 [12288, 8], P('dp', 'book'), may hold values from 0 to 2047
- master: float32 [8, 2048, 1024], P('book', 'dp'), may hold values from -5 to 5
- first_moment: float32 [8, 2048, 1024], P('book', 'dp'), may hold values from -6 to 6
- second_moment: float32 [8, 2048, 1024], P('book', 'dp'), may hold values from 1 to 30
Outputs:
- new_master: float32 [8, 2048, 1024], P('book', 'dp')
- new_first: float32 [8, 2048, 1024], P('book', 'dp')
- new_second: float32 [8, 2048, 1024], P('book', 'dp')
All inputs are finite; a program needn't handle non-finite values.
Results may differ from a plain program's by a relative error of at most 0.002.
Values may be sent and summed in bfloat16 or wider, within the bound.
A program may use at most 192 MiB of HBM per device.

v0:
```python
import jax
import jax.numpy as jnp
from jax import lax
from jax.sharding import PartitionSpec as P

STEPS = 2


def make_pull(corpus_rows, recon):
    values = corpus_rows.astype(jnp.float32)
    resid = values - recon
    unit = values * lax.rsqrt(jnp.sum(values * values, axis=-1, keepdims=True) + 1e-06)
    along = jnp.sum(resid * unit, axis=-1, keepdims=True)
    return (resid + 3.0 * along * unit).astype(jnp.bfloat16)


def per_device(corpus_rows, code_ids, master, first_moment, second_moment):
    book_count = master.shape[0]
    shard_rows = master.shape[1]
    width = master.shape[2]
    local_rows = corpus_rows.shape[0]
    for turn_index in range(STEPS):
        books = master.astype(jnp.bfloat16)
        empty = jnp.zeros((local_rows, width), jnp.float32)
        full_books = lax.all_gather(books, "dp", axis=1, tiled=True)
        partial_value = empty
        for book_slot in range(book_count):
            partial_value = partial_value + jnp.take(
                full_books[book_slot], code_ids[:, book_slot], axis=0
            ).astype(jnp.float32)
        recon = lax.psum(partial_value, "book")
        pull = make_pull(corpus_rows, recon)
        columns = lax.broadcasted_iota(jnp.int32, (1, lax.axis_size("dp") * shard_rows), 1)
        blocks = []
        for grad_book_slot in range(book_count):
            one_hot = (code_ids[:, grad_book_slot][:, None] == columns).astype(jnp.bfloat16)
            summed = lax.dot_general(
                one_hot, pull, (((0,), (0,)), ((), ())), preferred_element_type=jnp.float32
            )
            blocks.append(-2.0 * summed)
        grad_flat = lax.psum_scatter(
            jnp.concatenate(blocks, axis=1), "dp", scatter_dimension=0, tiled=True
        )
        grad = jnp.transpose(grad_flat.reshape(shard_rows, book_count, width), (1, 0, 2))
        first_moment = 0.9 * first_moment + 0.1 * grad
        second_moment = 0.99 * second_moment + 0.01 * grad * grad
        master = master - 0.05 * first_moment / (jnp.sqrt(second_moment) + 1e-08)
    return (master, first_moment, second_moment)


def solution(mesh):
    in_specs = (
        P("dp", None),
        P("dp", "book"),
        P("book", "dp", None),
        P("book", "dp", None),
        P("book", "dp", None),
    )
    out_specs = (P("book", "dp", None), P("book", "dp", None), P("book", "dp", None))
    return jax.shard_map(
        per_device, mesh=mesh, in_specs=in_specs, out_specs=out_specs, check_vma=False
    )
```

profile of v0, /device:TPU:0, one launch (start us, length us, event | category | flops | bytes accessed | tf_op | source)
XLA Modules:
  0.0 1295.0 jit_solution(10355159778973246720)
XLA Ops:
  7.2 0.0 all-gather.3.cloned.1.call-start
  7.2 2.7 convert_element_type.49
  9.9 0.0 all-gather.3.cloned.1.call-update
  10.0 0.0 all-reduce.3.cloned.1.call-start
  10.2 130.2 %all-gather.3.cloned.1.call-done = bf16[4,2048,1024]{2,1,0:T(8,128)(2,1)} async-done(((bf16[4,128,1024]{2,1,0:T(8,128)(2,1)}), bf16[4,2048,1024]{2,1,0:T(8,128)(2,1)}) %all-gather.3.cloned.1.call-update) | async-done | bytes 16777232 | tf_op jit(solution)/shard_map/all_gather | solution.py:25
  140.4 12.2 slice_bitcast_fusion.7
  152.6 6.5 gather_fusion
  159.2 6.5 gather_fusion.3
  165.7 7.3 gather_fusion.2
  173.0 7.3 gather_fusion.1
  180.3 4.0 convert_add_fusion.1
  184.3 0.2 reduce-scatter.3.cloned.1.call-start
  184.6 1.2 copy-done
  185.7 0.4 fusion.26
  186.1 82.3 %all-reduce.3.cloned.1.call-done = f32[768,1024]{1,0:T(8,128)} async-done(((f32[768,1024]{1,0:T(8,128)}), f32[768,1024]{1,0:T(8,128)}) %all-reduce.3.cloned.1.call-update) | async-done | bytes 3145744 | tf_op jit(solution)/shard_map/psum | solution.py:31
  268.4 2.8 fusion.20
  271.2 0.0 copy-done.2
  271.2 0.7 fusion.22
  271.9 3.8 fusion.18
  275.7 3.8 fusion.16
  279.5 6.2 fusion.14
  285.7 6.0 fusion.12
  291.7 18.8 %pad_maximum_fusion = f32[2048,4096]{0,1:T(8,128)} fusion(f32[2048,1024]{0,1:T(8,128)S(1)} %fusion.18, f32[2048,1024]{0,1:T(8,128)S(1)} %fusion.16, f32[2048,1024]{0,1:T(8,128)} %fusion.14, f32[2048,1024]{0,1:T(8,128)} %fusion.12), kind=kLoop, calls=%fused_computation.8 | loop fusion | flops 25165824 | bytes 67108864 | tf_op jit(solution)/shard_map/concatenate | solution.py:42
  310.6 0.0 all-gather.5.cloned.1.call-start
  310.6 332.9 %reduce-scatter.3.cloned.1.call-done = f32[128,4096]{0,1:T(8,128)} async-done(((f32[2048,4096]{0,1:T(8,128)}), f32[128,4096]{0,1:T(8,128)}) %reduce-scatter.3.cloned.1.call-update) | async-done | bytes 2097168 | tf_op jit(solution)/shard_map/reduce_scatter | solution.py:41
  643.5 2.9 copy.8
  646.4 6.5 fusion.41
  652.9 0.0 all-reduce.5.cloned.1.call-start
  652.9 126.0 %all-gather.5.cloned.1.call-done = bf16[4,2048,1024]{2,1,0:T(8,128)(2,1)} async-done(((bf16[4,128,1024]{2,1,0:T(8,128)(2,1)}), bf16[4,2048,1024]{2,1,0:T(8,128)(2,1)}) %all-gather.5.cloned.1.call-update) | async-done | bytes 16777232 | tf_op jit(solution)/shard_map/all_gather | solution.py:25
  778.9 12.6 slice_bitcast_fusion.3
  791.5 6.5 gather_fusion.4
  798.0 7.3 gather_fusion.7
  805.3 7.3 gather_fusion.6
  812.6 7.3 gather_fusion.5
  819.9 4.3 convert_add_fusion
  824.2 0.2 reduce-scatter.5.cloned.1.call-start
  824.5 83.9 %all-reduce.5.cloned.1.call-done = f32[768,1024]{1,0:T(8,128)} async-done(((f32[768,1024]{1,0:T(8,128)}), f32[768,1024]{1,0:T(8,128)}) %all-reduce.5.cloned.1.call-update) | async-done | bytes 3145744 | tf_op jit(solution)/shard_map/psum | solution.py:31
  908.3 2.8 fusion.23
  911.1 0.0 copy-done.3
  911.2 0.7 fusion.25
  911.9 3.8 fusion.19
  915.6 3.8 fusion.17
  919.4 4.0 fusion.15
  923.4 6.0 fusion.13
  929.4 14.9 %pad_maximum_fusion.1 = f32[2048,4096]{0,1:T(8,128)} fusion(f32[2048,1024]{0,1:T(8,128)S(1)} %fusion.19, f32[2048,1024]{0,1:T(8,128)S(1)} %fusion.17, f32[2048,1024]{0,1:T(8,128)S(1)} %fusion.15, f32[2048,1024]{0,1:T(8,128)} %fusion.13), kind=kLoop, calls=%fused_computation.9 | loop fusion | flops 25165824 | bytes 67108864 | tf_op jit(solution)/shard_map/concatenate | solution.py:42
  944.3 332.9 %reduce-scatter.5.cloned.1.call-done = f32[128,4096]{0,1:T(8,128)} async-done(((f32[2048,4096]{0,1:T(8,128)}), f32[128,4096]{0,1:T(8,128)}) %reduce-scatter.5.cloned.1.call-update) | async-done | bytes 2097168 | tf_op jit(solution)/shard_map/reduce_scatter | solution.py:41
  1277.2 3.0 copy.9
  1280.3 7.6 divide_subtract_fusion
  (24 shorter events, 0.2 us)
Async XLA Ops:
  7.2 2.9 copy-start.4
  7.2 133.3 %all-gather.3.cloned.1.call-start = ((), (), s32[]{:S(2)}) async-start(), calls=%async_computation.2 | async-start | bytes 17825792 | tf_op jit(solution)/shard_map/all_gather | solution.py:25
  10.0 258.4 %all-reduce.3.cloned.1.call-start = ((), (), s32[]{:S(2)}) async-start(), calls=%async_computation.3 | async-start | bytes 6291456 | tf_op jit(solution)/shard_map/psum | solution.py:31
  184.3 1.4 copy-start
  184.3 459.1 %reduce-scatter.3.cloned.1.call-start = ((), (), s32[]{:S(2)}) async-start(), calls=%async_computation.4 | async-start | bytes 35651584 | tf_op jit(solution)/shard_map/reduce_scatter | solution.py:41
  268.4 2.8 copy-start.2
  310.6 468.4 %all-gather.5.cloned.1.call-start = ((), (), s32[]{:S(2)}) async-start(), calls=%async_computation.5 | async-start | bytes 17825792 | tf_op jit(solution)/shard_map/all_gather | solution.py:25
  652.9 255.5 %all-reduce.5.cloned.1.call-start = ((), (), s32[]{:S(2)}) async-start(), calls=%async_computation.6 | async-start | bytes 6291456 | tf_op jit(solution)/shard_map/psum | solution.py:31
  824.2 453.0 %reduce-scatter.5.cloned.1.call-start = ((), (), s32[]{:S(2)}) async-start(), calls=%async_computation.7 | async-start | bytes 35651584 | tf_op jit(solution)/shard_map/reduce_scatter | solution.py:41
  908.3 2.8 copy-start.3
  1277.2 3.0 copy-start.1
Sparse Core Ops, SparseCore 0:
  10.8 129.6 all-gather.2
  184.5 83.9 all-reduce.2
  310.7 332.7 reduce-scatter.2
  653.0 125.9 all-gather.4
  824.4 83.9 all-reduce.4
  944.5 332.7 reduce-scatter.4
where the time goes:
time: 1300 us; the launch traced here: 1290 us
  waiting for transfers between devices  1090 us (84%)
  local copies, waits for them, and re-layouts  88 us (7%)
  other arithmetic  66.3 us (5%)
  matrix products  37.3 us (3%)
  between operations  14.5 us (1%)
    reduce_scatter x2, waiting for transfers between devices, per_device(): lax.psum_scatter(jnp.concatenate(blocks, axis=1), 'dp', scatter_dimension...  666 us
    all_gather x2, waiting for transfers between devices, per_device(): full_books = lax.all_gather(books, 'dp', axis=1, tiled=True)  256 us
    psum x2, waiting for transfers between devices, per_device(): recon = lax.psum(partial_value, 'book')  166 us
    gather x8, local copies, waits for them, and re-layouts, per_device(): jnp.take(full_books[book_slot], code_ids[:, book_slot], axis=0)  56 us
    dot_general x8, matrix products, per_device(): lax.dot_general(one_hot, pull, (((0,), (0,)), ((), ())), preferred_elemen...  37.3 us
    concatenate x2, other arithmetic, per_device(): jnp.concatenate(blocks, axis=1)  33.7 us
  transfers between devices with their start and end apart: 6, of which 6 were waited for; matrix products, arithmetic and copies ran while one was open for 0% of the time, Pallas kernels for 0%

commit v1 on v0

v1 whole, which is shorter than its diff:
```python
import functools

import jax
import jax.numpy as jnp
from jax import lax
from jax.experimental import pallas as pl
from jax.experimental.pallas import tpu as pltpu
from jax.sharding import PartitionSpec as P

STEPS = 2
LOW = 256
CHUNK = 1024
AXES = ("dp", "book")


def one_hot_of(low_ids, chunk):
    places = lax.broadcasted_iota(jnp.int32, (LOW, chunk), 0)
    return (places == low_ids).astype(jnp.float32).astype(jnp.bfloat16)


def recon_kernel(ids_ref, table_ref, corpus_ref, resid_ref, dots_ref):
    books = ids_ref.shape[0]
    chunk = ids_ref.shape[1]
    cols = corpus_ref.shape[0]
    values = corpus_ref[...].astype(jnp.float32)
    total = jnp.zeros((cols, chunk), jnp.float32)
    for m in range(books):
        ids = ids_ref[m : m + 1, :]
        high = ids // LOW
        picked = jnp.dot(
            table_ref[m], one_hot_of(ids - high * LOW, chunk), preferred_element_type=jnp.float32
        )
        for g in range(table_ref.shape[1] // cols):
            total = total + jnp.where(high == g, picked[g * cols : (g + 1) * cols, :], 0.0)
    resid = values - total
    resid_ref[...] = resid
    dots_ref[0:1, :] = jnp.sum(resid * values, axis=0, keepdims=True)
    dots_ref[1:2, :] = jnp.sum(values * values, axis=0, keepdims=True)


def grad_kernel(ids_ref, resid_ref, corpus_ref, dots_ref, grad_ref):
    books = ids_ref.shape[0]
    chunk = ids_ref.shape[1]
    cols = corpus_ref.shape[0]
    groups = grad_ref.shape[1] // cols

    @pl.when(pl.program_id(0) == 0)
    def _():
        grad_ref[...] = jnp.zeros_like(grad_ref)

    values = corpus_ref[...].astype(jnp.float32)
    scale = lax.rsqrt(dots_ref[1:2, :] + 1e-06)
    along = dots_ref[0:1, :] * scale
    pull = (resid_ref[...] + 3.0 * along * (values * scale)).astype(jnp.bfloat16)
    pull = -2.0 * pull.astype(jnp.float32)
    for m in range(books):
        ids = ids_ref[m : m + 1, :]
        high = ids // LOW
        spread = jnp.concatenate(
            [jnp.where(high == g, pull, 0.0).astype(jnp.bfloat16) for g in range(groups)], axis=0
        )
        grad_ref[m] += lax.dot_general(
            spread,
            one_hot_of(ids - high * LOW, chunk),
            (((1,), (1,)), ((), ())),
            preferred_element_type=jnp.float32,
        )


def run_recon(ids, table, corpus):
    books, tokens = ids.shape
    cols = corpus.shape[0]
    by_token = lambda rows: pl.BlockSpec((rows, CHUNK), lambda i: (0, i))
    whole = pl.BlockSpec(table.shape, lambda i: (0, 0, 0))
    return pl.pallas_call(
        recon_kernel,
        grid=(tokens // CHUNK,),
        in_specs=[by_token(books), whole, by_token(cols)],
        out_specs=[by_token(cols), by_token(2)],
        out_shape=[
            jax.ShapeDtypeStruct((cols, tokens), jnp.float32),
            jax.ShapeDtypeStruct((2, tokens), jnp.float32),
        ],
        compiler_params=pltpu.CompilerParams(vmem_limit_bytes=48 * 2**20),
    )(ids, table, corpus)


def run_grad(ids, resid, corpus, dots, groups):
    books, tokens = ids.shape
    cols = corpus.shape[0]
    by_token = lambda rows: pl.BlockSpec((rows, CHUNK), lambda i: (0, i))
    out = (books, groups * cols, LOW)
    return pl.pallas_call(
        grad_kernel,
        grid=(tokens // CHUNK,),
        in_specs=[by_token(books), by_token(cols), by_token(cols), by_token(2)],
        out_specs=pl.BlockSpec(out, lambda i: (0, 0, 0)),
        out_shape=jax.ShapeDtypeStruct(out, jnp.float32),
        compiler_params=pltpu.CompilerParams(vmem_limit_bytes=48 * 2**20),
    )(ids, resid, corpus, dots)


def per_device(corpus_rows, code_ids, master, first_moment, second_moment):
    local_books, shard, width = master.shape
    local_rows = corpus_rows.shape[0]
    dp, book = lax.axis_size("dp"), lax.axis_size("book")
    devices = dp * book
    cols = width // devices
    padded = max(cols, 16)
    books, codes, tokens = local_books * book, shard * dp, local_rows * dp
    groups = codes // LOW

    def pad_cols(array, axis):
        widths = [(0, 0)] * array.ndim
        widths[axis] = (0, padded - cols)
        return jnp.pad(array, widths) if padded > cols else array

    ids = lax.all_gather(code_ids.T, AXES, axis=0)
    ids = ids.reshape(dp, book, local_books, local_rows).transpose(1, 2, 0, 3).reshape(books, tokens)

    mine = lax.dynamic_index_in_dim(
        corpus_rows.reshape(local_rows, dp, book, cols), lax.axis_index("book"), 2, keepdims=False
    )
    corpus = lax.all_to_all(mine.transpose(1, 2, 0), "dp", 0, 0)
    corpus = pad_cols(corpus.transpose(1, 0, 2).reshape(cols, tokens), 0)

    for _ in range(STEPS):
        outgoing = master.astype(jnp.bfloat16).reshape(local_books, shard, devices, cols)
        incoming = lax.all_to_all(outgoing.transpose(2, 0, 3, 1), AXES, 0, 0)
        table = incoming.reshape(dp, book, local_books, cols, shard).transpose(1, 2, 3, 0, 4)
        table = table.reshape(books, cols, groups, LOW).transpose(0, 2, 1, 3)
        table = pad_cols(table, 2).reshape(books, groups * padded, LOW)
        resid, dots = run_recon(ids, table, corpus)
        dots = lax.psum(dots, AXES)
        grad = run_grad(ids, resid, corpus, dots, groups)
        grad = grad.reshape(books, groups, padded, LOW)[:, :, :cols].transpose(0, 2, 1, 3)
        grad = grad.reshape(book, local_books, cols, dp, shard).transpose(3, 0, 1, 2, 4)
        grad = lax.all_to_all(grad.reshape(devices, local_books, cols, shard), AXES, 0, 0)
        grad = grad.transpose(1, 3, 0, 2).reshape(local_books, shard, width)
        first_moment = 0.9 * first_moment + 0.1 * grad
        second_moment = 0.99 * second_moment + 0.01 * grad * grad
        master = master - 0.05 * first_moment / (jnp.sqrt(second_moment) + 1e-08)
    return (master, first_moment, second_moment)


def solution(mesh):
    state = P("book", "dp", None)
    return jax.shard_map(
        per_device,
        mesh=mesh,
        in_specs=(P("dp", None), P("dp", "book"), state, state, state),
        out_specs=(state, state, state),
        check_vma=False,
    )
```

time: 1300 us -> 631 us (0.49)
  waiting for transfers between devices: 1090 us -> 297 us
  blocking collectives: 0 us -> 165 us
  Pallas kernels: 0 us -> 88.7 us
  other arithmetic: 66.3 us -> 6.64 us
  local copies, waits for them, and re-layouts: 88 us -> 40.3 us
  matrix products: 37.3 us -> 0 us
  starting transfers between devices: 0.59 us -> 18.4 us
    reduce_scatter x2 -> x0, waiting for transfers between devices: 666 us -> none  [per_device(): lax.psum_scatter(jnp.concatenate(blocks, axis=1), 'dp', scatter_dimension...]
    all_gather x2 -> x0, waiting for transfers between devices: 256 us -> none  [per_device(): full_books = lax.all_gather(books, 'dp', axis=1, tiled=True)]
    pallas_call x0 -> x4, Pallas kernels: none -> 88.7 us  [the longest x2 56 us: run_recon(): pl.pallas_call(recon_kernel, grid=(tokens // CHUNK,), in_specs=[by_token(...]
    all_to_all x0 -> x2, blocking collectives: none -> 83.7 us  [the longest x1 53.9 us: per_device(): lax.all_to_all(grad.reshape(devices, local_books, cols, shard), AXES, 0, 0)]
    all_gather x0 -> x1, blocking collectives: none -> 81.4 us  [per_device(): ids = lax.all_gather(code_ids.T, AXES, axis=0)]
    psum x2, waiting for transfers between devices: 166 us -> 238 us  [per_device(): dots = lax.psum(dots, AXES)]
    all_to_all x0 -> x3, waiting for transfers between devices: none -> 58.2 us  [the longest x1 43.1 us: per_device(): lax.all_to_all(grad.reshape(devices, local_books, cols, shard), AXES, 0, 0)]
    gather x8 -> x0, local copies, waits for them, and re-layouts: 56 us -> none  [per_device(): jnp.take(full_books[book_slot], code_ids[:, book_slot], axis=0)]
  transfers between devices with their start and end apart: 6 -> 5, of which waited for: 6 -> 4; matrix products, arithmetic and copies ran while one was open for 0% -> 1% of each run, Pallas kernels for 0% -> 0%
where the time goes in v1:
time: 631 us; the launch traced here: 630 us
  waiting for transfers between devices  297 us (47%)
  blocking collectives  165 us (26%)
  Pallas kernels  88.7 us (14%)
  local copies, waits for them, and re-layouts  40.3 us (6%)
  starting transfers between devices  18.4 us (3%)
  between operations  14.3 us (2%)
  other arithmetic  6.64 us (1%)
    psum x2, waiting for transfers between devices, per_device(): dots = lax.psum(dots, AXES)  238 us
    all_gather x1, blocking collectives, per_device(): ids = lax.all_gather(code_ids.T, AXES, axis=0)  81.4 us
    pallas_call x2, Pallas kernels, run_recon(): pl.pallas_call(recon_kernel, grid=(tokens // CHUNK,), in_specs=[by_token(...  56 us
    all_to_all x1, blocking collectives, per_device(): lax.all_to_all(grad.reshape(devices, local_books, cols, shard), AXES, 0, 0)  53.9 us
    all_to_all x1, waiting for transfers between devices, per_device(): lax.all_to_all(grad.reshape(devices, local_books, cols, shard), AXES, 0, 0)  43.1 us
    pallas_call x2, Pallas kernels, run_grad(): pl.pallas_call(grad_kernel, grid=(tokens // CHUNK,), in_specs=[by_token(b...  32.7 us
    all_to_all x1, blocking collectives, per_device(): incoming = lax.all_to_all(outgoing.transpose(2, 0, 3, 1), AXES, 0, 0)  29.7 us
    unnamed x32, local copies, waits for them, and re-layouts  21.9 us
  transfers between devices with their start and end apart: 5, of which 4 were waited for; matrix products, arithmetic and copies ran while one was open for 1% of the time, Pallas kernels for 0%

profile of v1, /device:TPU:0, one launch (start us, length us, event | category | flops | bytes accessed | tf_op | source)
XLA Modules:
  0.0 630.1 jit_solution(4153237863416790800)
XLA Ops:
  7.2 1.7 copy.51
  8.9 1.0 dynamic-slice_bitcast_fusion
  9.8 7.4 %all-to-all-start.1 = ((bf16[16,32,768]{2,1,0:T(8,128)(2,1)}), bf16[16,32,768]{2,1,0:T(8,128)(2,1)S(1)}, u32[]{:S(2)}, u32[]{:S(2)}) async-start(bf16[16,32,768]{2,1,0:T(8,128)(2,1)} %dynamic-slice_bitcast_fusion), calls=%async_computation.1 | async-start | bytes 1572864 | tf_op jit(solution)/shard_map/all_to_all | solution.py:124
  17.2 1.9 copy.57
  19.2 0.1 convert_element_type.6
  19.3 1.3 copy.48
  20.6 0.2 copy-done.2
  20.8 15.1 %all-to-all-done.1 = bf16[16,32,768]{2,1,0:T(8,128)(2,1)S(1)} async-done(((bf16[16,32,768]{2,1,0:T(8,128)(2,1)}), bf16[16,32,768]{2,1,0:T(8,128)(2,1)S(1)}, u32[]{:S(2)}, u32[]{:S(2)}) %all-to-all-start.1) | async-done | bytes 786464 | tf_op jit(solution)/shard_map/all_to_all | solution.py:124
  35.9 5.4 all-to-all-start
  41.4 81.4 %all-gather.1 = s32[32,4,768]{2,1,0:T(4,128)S(1)} all-gather(s32[1,4,768]{2,1,0:T(4,128)S(1)} %bitcast.109), channel_id=2, replica_groups=mesh['dp'=16,'book'=2] {'dp','book'}, dimensions={0}, use_global_device_ids=true | all-gather | bytes 405504 | tf_op jit(solution)/shard_map/all_gather | solution.py:118
  122.9 0.2 copy.68
  123.2 0.7 copy.76
  123.9 0.4 reshape.70
  124.3 0.3 copy.50
  124.6 28.0 %shard_map.76 = (f32[32,12288]{1,0:T(8,128)S(1)}, f32[2,12288]{1,0:T(2,128)}) custom-call(s32[8,12288]{1,0:T(8,128)S(1)} %bitcast.83, bf16[8,256,256]{2,1,0:T(8,128)(2,1)S(1)} %bitcast.89, bf16[32,12288]{1,0:T(8,128)(2,1)S(1)} %bitcast.79), custom_call_target="tpu_custom_call" | custom-call | tf_op jit(solution)/shard_map/pallas_call | solution.py:75
  152.6 118.7 %all-reduce.3.cloned.1.call-done.dots_ref = f32[2,12288]{1,0:T(2,128)} async-done(((f32[2,12288]{1,0:T(2,128)}), f32[2,12288]{1,0:T(2,128)}) %all-reduce.3.cloned.1.call-update) | async-done | bytes 98320 | tf_op jit(solution)/shard_map/psum | solution.py:134
  271.3 0.9 copy-done.1
  272.2 16.3 %shard_map.77 = f32[8,256,256]{2,1,0:T(8,128)S(1)} custom-call(s32[8,12288]{1,0:T(8,128)S(1)} %bitcast.84, f32[32,12288]{1,0:T(8,128)S(1)} %get-tuple-element.7.resid_ref, bf16[32,12288]{1,0:T(8,128)(2,1)S(1)} %bitcast.80, f32[2,12288]{1,0:T(2,128)S(1)} %copy-done.1), custom_call_target="tpu_custom_call" | custom-call | tf_op jit(solution)/shard_map/pallas_call | solution.py:93
  288.6 1.2 copy.74
  289.8 1.4 reshape.75
  291.2 3.6 copy.54
  294.8 5.6 all-to-all-start.2
  300.4 1.9 copy.45
  302.3 3.6 copy.56
  306.0 43.1 %all-to-all-done.2 = f32[32,4,32,128]{3,2,1,0:T(8,128)} async-done(((f32[32,4,32,128]{3,2,1,0:T(8,128)}), f32[32,4,32,128]{3,2,1,0:T(8,128)}, u32[]{:S(2)}, u32[]{:S(2)}) %all-to-all-start.2) | async-done | bytes 2097184 | tf_op jit(solution)/shard_map/all_to_all | solution.py:138
  349.0 1.9 copy.55
  351.0 0.3 copy-done.3
  351.3 0.6 copy-done.6
  351.9 2.7 fusion.6
  354.8 29.7 %all_to_all.25 = bf16[32,4,32,128]{3,2,1,0:T(8,128)(2,1)S(1)} all-to-all(bf16[32,4,32,128]{3,2,1,0:T(8,128)(2,1)S(1)} %copy.58), channel_id=1, replica_groups=mesh['dp'=16,'book'=2] {'dp','book'}, dimensions={0} | all-to-all | bytes 2097152 | tf_op jit(solution)/shard_map/all_to_all | solution.py:129
  384.5 0.7 copy.75
  385.2 0.4 reshape.80
  385.6 0.3 copy.60
  385.8 28.0 %shard_map.78 = (f32[32,12288]{1,0:T(8,128)S(1)}, f32[2,12288]{1,0:T(2,128)}) custom-call(s32[8,12288]{1,0:T(8,128)S(1)} %bitcast.85, bf16[8,256,256]{2,1,0:T(8,128)(2,1)S(1)} %bitcast.90, bf16[32,12288]{1,0:T(8,128)(2,1)S(1)} %bitcast.81), custom_call_target="tpu_custom_call" | custom-call | tf_op jit(solution)/shard_map/pallas_call | solution.py:75
  413.9 119.7 %all-reduce.5.cloned.1.call-done.dots_ref = f32[2,12288]{1,0:T(2,128)} async-done(((f32[2,12288]{1,0:T(2,128)}), f32[2,12288]{1,0:T(2,128)}) %all-reduce.5.cloned.1.call-update) | async-done | bytes 98320 | tf_op jit(solution)/shard_map/psum | solution.py:134
  533.6 0.9 copy-done
  534.5 16.3 %shard_map.79 = f32[8,256,256]{2,1,0:T(8,128)S(1)} custom-call(s32[8,12288]{1,0:T(8,128)S(1)} %bitcast.86, f32[32,12288]{1,0:T(8,128)S(1)} %get-tuple-element.9.resid_ref, bf16[32,12288]{1,0:T(8,128)(2,1)S(1)} %bitcast.82, f32[2,12288]{1,0:T(2,128)S(1)} %copy-done), custom_call_target="tpu_custom_call" | custom-call | tf_op jit(solution)/shard_map/pallas_call | solution.py:93
  550.8 1.2 copy.73
  552.0 1.4 reshape.83
  553.4 2.3 copy.62
  555.7 53.9 %all_to_all.26 = f32[32,4,32,128]{3,2,1,0:T(8,128)S(1)} all-to-all(f32[32,4,32,128]{3,2,1,0:T(8,128)S(1)} %bitcast.95), channel_id=1, replica_groups=mesh['dp'=16,'book'=2] {'dp','book'}, dimensions={0} | all-to-all | bytes 4194304 | tf_op jit(solution)/shard_map/all_to_all | solution.py:138
  609.7 0.2 copy.63
  609.9 1.3 copy-done.5
  611.3 0.6 copy-done.7
  611.9 3.8 divide_subtract_fusion
  615.7 2.9 copy.64
  618.6 2.9 copy.65
  621.4 1.8 copy.66
  (25 shorter events, 0.5 us)
Async XLA Ops:
  9.8 26.1 %all-to-all-start.1 = ((bf16[16,32,768]{2,1,0:T(8,128)(2,1)}), bf16[16,32,768]{2,1,0:T(8,128)(2,1)S(1)}, u32[]{:S(2)}, u32[]{:S(2)}) async-start(bf16[16,32,768]{2,1,0:T(8,128)(2,1)} %dynamic-slice_bitcast_fusion), calls=%async_computation.1 | async-start | bytes 1572864 | tf_op jit(solution)/shard_map/all_to_all | solution.py:124
  19.2 1.7 copy-start.2
  19.3 22.1 %copy-start.11 = (s32[768,4]{0,1:T(4,128)S(1)}, s32[768,4]{0,1:T(4,128)}, u32[]{:S(2)}) copy-start(s32[768,4]{0,1:T(4,128)} %param.6) | copy-start | bytes 36868
  35.9 87.3 %all-to-all-start = ((bf16[32,4,32,128]{3,2,1,0:T(8,128)(2,1)}), bf16[32,4,32,128]{3,2,1,0:T(8,128)(2,1)S(1)}, u32[]{:S(2)}, u32[]{:S(2)}) async-start(bf16[32,4,32,128]{3,2,1,0:T(8,128)(2,1)} %copy.48), calls=%async_computation | async-start | bytes 2097152 | tf_op jit(solution)/shard_map/all_to_all | solution.py:129
  41.3 230.0 %all-reduce.3.cloned.1.call-start = ((), (), s32[]{:S(2)}) async-start(), calls=%async_computation.5 | async-start | bytes 196608 | tf_op jit(solution)/shard_map/psum | solution.py:134
  271.3 0.9 copy-start.1
  294.8 54.3 %all-to-all-start.2 = ((f32[32,4,32,128]{3,2,1,0:T(8,128)}), f32[32,4,32,128]{3,2,1,0:T(8,128)}, u32[]{:S(2)}, u32[]{:S(2)}) async-start(f32[32,4,32,128]{3,2,1,0:T(8,128)} %bitcast.17), calls=%async_computation.2 | async-start | bytes 4194304 | tf_op jit(solution)/shard_map/all_to_all | solution.py:138
  300.3 233.3 %all-reduce.5.cloned.1.call-start = ((), (), s32[]{:S(2)}) async-start(), calls=%async_computation.6 | async-start | bytes 196608 | tf_op jit(solution)/shard_map/psum | solution.py:134
  302.3 48.7 %copy-start.4 = (f32[4,128,1024]{1,2,0:T(8,128)}, f32[4,128,1024]{1,2,0:T(8,128)S(1)}, u32[]{:S(2)}) copy-start(f32[4,128,1024]{1,2,0:T(8,128)S(1)} %copy.45) | copy-start | bytes 6291460
  349.0 2.2 copy-start.3
  349.0 2.9 copy-start.6
  351.9 2.7 copy-start.8
  533.6 0.9 copy-start
  555.7 54.2 %copy-start.9 = (f32[4,128,32,32]{1,3,2,0:T(8,128)S(1)}, f32[4,128,32,32]{1,3,2,0:T(8,128)}, u32[]{:S(2)}) copy-start(f32[4,128,32,32]{1,3,2,0:T(8,128)} %copy-done.8) | copy-start | bytes 6291460
  555.7 54.2 %copy-start.10 = (f32[4,128,1024]{1,2,0:T(8,128)S(1)}, f32[4,128,1024]{1,2,0:T(8,128)}, u32[]{:S(2)}) copy-start(f32[4,128,1024]{1,2,0:T(8,128)} %get-tuple-element.24) | copy-start | bytes 6291460
  609.7 1.6 copy-start.5
  609.7 2.2 copy-start.7
Sparse Core Ops, SparseCore 0:
  152.7 118.5 all-reduce.2
  414.0 119.5 all-reduce.4

commit v2 on v1

v2 whole, which is shorter than its diff:
```python
import functools
import math

import jax
import jax.numpy as jnp
from jax import lax
from jax.experimental import pallas as pl
from jax.experimental.pallas import tpu as pltpu
from jax.sharding import PartitionSpec as P

STEPS = 2
LOW = 256
CHUNK = 1024
PARTS = 1
AXES = ("dp", "book")
VMEM = 48 * 2**20


def one_hot_of(low_ids, chunk):
    places = lax.broadcasted_iota(jnp.int32, (LOW, chunk), 0).astype(jnp.float32).astype(jnp.bfloat16)
    ids = low_ids.astype(jnp.float32).astype(jnp.bfloat16)
    return jnp.where(places == ids, jnp.bfloat16(1), jnp.bfloat16(0))


def recon_kernel(ids_ref, table_ref, corpus_ref, before_ref, resid_ref, dots_ref):
    books = ids_ref.shape[0]
    chunk = ids_ref.shape[1]
    cols = corpus_ref.shape[0]
    total = before_ref[...].astype(jnp.float32)
    for m in range(books):
        ids = ids_ref[m : m + 1, :]
        high = ids // LOW
        picked = jnp.dot(
            table_ref[m], one_hot_of(ids - high * LOW, chunk), preferred_element_type=jnp.float32
        )
        for g in range(table_ref.shape[1] // cols):
            total = total - jnp.where(high == g, picked[g * cols : (g + 1) * cols, :], 0.0)
    resid_ref[...] = total
    values = corpus_ref[...].astype(jnp.float32)
    dots_ref[...] = jnp.sum(total * values, axis=0, keepdims=True)


def grad_kernel(shrink, ids_ref, resid_ref, corpus_ref, coef_ref, out_ref, grad_ref):
    books = ids_ref.shape[0]
    chunk = ids_ref.shape[1]
    cols = corpus_ref.shape[0]
    groups = grad_ref.shape[1] // cols

    @pl.when(pl.program_id(0) == 0)
    def _():
        grad_ref[...] = jnp.zeros_like(grad_ref)

    values = corpus_ref[...].astype(jnp.float32)
    pull = (resid_ref[...] + coef_ref[...] * values).astype(jnp.bfloat16).astype(jnp.float32)
    for m in range(books):
        ids = ids_ref[m : m + 1, :]
        high = ids // LOW
        spread = jnp.concatenate(
            [jnp.where(high == g, pull, 0.0).astype(jnp.bfloat16) for g in range(groups)], axis=0
        )
        grad_ref[m] += lax.dot_general(
            spread,
            one_hot_of(ids - high * LOW, chunk),
            (((1,), (1,)), ((), ())),
            preferred_element_type=jnp.float32,
        )

    @pl.when(pl.program_id(0) == pl.num_programs(0) - 1)
    def _():
        out_ref[...] = (grad_ref[...] * (-2.0 * shrink)).astype(out_ref.dtype)


def adam_kernel(grow, grad_ref, master_ref, first_ref, second_ref, *outs):
    width, shard = master_ref.shape[2], master_ref.shape[1]
    sent = grad_ref[...].astype(jnp.float32).reshape(width, shard) * grow
    grad = sent.T
    first = 0.9 * first_ref[0] + 0.1 * grad
    second = 0.99 * second_ref[0] + 0.01 * grad * grad
    master = master_ref[0] - 0.05 * first / (jnp.sqrt(second) + 1e-08)
    outs[0][0] = master
    outs[1][0] = first
    outs[2][0] = second
    if len(outs) > 3:
        outs[3][...] = master.T.astype(jnp.bfloat16).reshape(outs[3].shape)


def run_recon(ids, table, corpus, before):
    books, tokens = ids.shape
    cols = corpus.shape[0]
    by_token = lambda rows: pl.BlockSpec((rows, CHUNK), lambda i: (0, i))
    whole = pl.BlockSpec(table.shape, lambda i: (0, 0, 0))
    return pl.pallas_call(
        recon_kernel,
        grid=(tokens // CHUNK,),
        in_specs=[by_token(books), whole, by_token(cols), by_token(cols)],
        out_specs=[by_token(cols), by_token(1)],
        out_shape=[
            jax.ShapeDtypeStruct((cols, tokens), jnp.float32),
            jax.ShapeDtypeStruct((1, tokens), jnp.float32),
        ],
        cost_estimate=pl.CostEstimate(
            flops=2 * books * tokens * LOW * table.shape[1], bytes_accessed=10 * cols * tokens, transcendentals=0
        ),
        compiler_params=pltpu.CompilerParams(vmem_limit_bytes=VMEM),
        name="lookup",
    )(ids, table, corpus, before)


def run_grad(ids, resid, corpus, coef, groups, shrink):
    books, tokens = ids.shape
    cols = corpus.shape[0]
    by_token = lambda rows: pl.BlockSpec((rows, CHUNK), lambda i: (0, i))
    out = (books, groups * cols, LOW)
    return pl.pallas_call(
        functools.partial(grad_kernel, shrink),
        grid=(tokens // CHUNK,),
        in_specs=[by_token(books), by_token(cols), by_token(cols), by_token(1)],
        out_specs=pl.BlockSpec(out, lambda i: (0, 0, 0)),
        out_shape=jax.ShapeDtypeStruct(out, jnp.float32),
        scratch_shapes=[pltpu.VMEM(out, jnp.float32)],
        cost_estimate=pl.CostEstimate(
            flops=2 * books * tokens * LOW * groups * cols, bytes_accessed=10 * cols * tokens, transcendentals=0
        ),
        compiler_params=pltpu.CompilerParams(vmem_limit_bytes=VMEM),
        name="scatter",
    )(ids, resid, corpus, coef)


def run_adam(grad, master, first, second, grow, again):
    sources, books, rows, shard = grad.shape
    state = pl.BlockSpec((1,) + master.shape[1:], lambda i: (i, 0, 0))
    moved = pl.BlockSpec((sources, 1, rows, shard), lambda i: (0, i, 0, 0))
    shapes = [jax.ShapeDtypeStruct(master.shape, jnp.float32)] * 3
    specs = [state] * 3
    if again:
        shapes = shapes + [jax.ShapeDtypeStruct(grad.shape, jnp.bfloat16)]
        specs = specs + [moved]
    return pl.pallas_call(
        functools.partial(adam_kernel, grow),
        grid=(books,),
        in_specs=[moved, state, state, state],
        out_specs=specs,
        out_shape=shapes,
        cost_estimate=pl.CostEstimate(
            flops=20 * master.size, bytes_accessed=28 * master.size, transcendentals=master.size
        ),
        compiler_params=pltpu.CompilerParams(vmem_limit_bytes=VMEM),
        name="adam",
    )(grad, master, first, second)


def per_device(corpus_rows, code_ids, master, first_moment, second_moment):
    local_books, shard, width = master.shape
    local_rows = corpus_rows.shape[0]
    dp, book = lax.axis_size("dp"), lax.axis_size("book")
    devices = dp * book
    cols = width // devices
    padded = max(cols, 16)
    parts = PARTS if local_books % PARTS == 0 else 1
    part_books = local_books // parts
    books, codes, tokens = part_books * book, shard * dp, local_rows * dp
    groups = codes // LOW
    bound = 2.0 * tokens * (54.0 + 3.0 * 54.0 * math.sqrt(width))
    shrink = 2.0 ** -max(0, math.ceil(math.log2(bound / 65000.0)))

    def pad_cols(array, axis):
        widths = [(0, 0)] * array.ndim
        widths[axis] = (0, padded - cols)
        return jnp.pad(array, widths) if padded > cols else array

    def to_blocks(moved):
        if cols >= 16:
            return moved
        return moved.transpose(1, 0, 2, 3).reshape(1, moved.shape[1], width, shard)

    def exchange(array):
        return lax.all_to_all(array, AXES, 0, 0)

    def books_out(part):
        cut = part.astype(jnp.bfloat16).reshape(part_books, shard, devices, cols)
        return cut.transpose(2, 0, 3, 1)

    split = lambda array: [array[p * part_books : (p + 1) * part_books] for p in range(parts)]
    masters, firsts, seconds = split(master), split(first_moment), split(second_moment)

    sent_ids = jnp.broadcast_to(code_ids.T.astype(jnp.int16)[None], (devices, local_books, local_rows))
    ids = exchange(sent_ids).astype(jnp.int32)
    ids = ids.reshape(dp, book, parts, part_books, local_rows).transpose(2, 1, 3, 0, 4)
    ids = ids.reshape(parts, books, tokens)

    mine = lax.dynamic_index_in_dim(
        corpus_rows.reshape(local_rows, dp, book, cols), lax.axis_index("book"), 2, keepdims=False
    )
    corpus = lax.all_to_all(mine.transpose(1, 2, 0), "dp", 0, 0)
    corpus = pad_cols(corpus.transpose(1, 0, 2).reshape(cols, tokens), 0)

    values = corpus_rows.astype(jnp.float32)
    squares = jnp.sum(values * values, axis=-1).reshape(book, local_rows // book)
    squares = lax.dynamic_index_in_dim(squares, lax.axis_index("book"), 0, keepdims=False)

    outgoing = [books_out(part) for part in masters]
    for turn in range(STEPS):
        resid = corpus
        for p in range(parts):
            incoming = exchange(outgoing[p])
            table = incoming.reshape(dp, book, part_books, cols, shard).transpose(1, 2, 3, 0, 4)
            table = table.reshape(books, cols, groups, LOW).transpose(0, 2, 1, 3)
            table = pad_cols(table, 2).reshape(books, groups * padded, LOW)
            resid, dots = run_recon(ids[p], table, corpus, resid)
        dots = jnp.sum(exchange(dots.reshape(devices, tokens // devices)), axis=0)
        coef = 3.0 * dots / (squares + 1e-06)
        coef = exchange(jnp.broadcast_to(coef[None], (devices, tokens // devices))).reshape(1, tokens)
        again = turn + 1 < STEPS
        outgoing = []
        for p in range(parts):
            grad = run_grad(ids[p], resid, corpus, coef, groups, shrink)
            grad = grad.reshape(books, groups, padded, LOW)[:, :, :cols].transpose(0, 2, 1, 3).astype(jnp.float16)
            grad = grad.reshape(book, part_books, cols, dp, shard).transpose(3, 0, 1, 2, 4)
            grad = exchange(grad.reshape(devices, part_books, cols, shard))
            out = run_adam(to_blocks(grad).astype(jnp.float32), masters[p], firsts[p], seconds[p], 1.0 / shrink, again)
            masters[p], firsts[p], seconds[p] = out[:3]
            if again:
                moved = out[3]
                if moved.shape[0] != devices:
                    moved = moved.reshape(part_books, devices, cols, shard).transpose(1, 0, 2, 3)
                outgoing.append(moved)
    join = lambda pieces: pieces[0] if parts == 1 else jnp.concatenate(pieces, axis=0)
    return (join(masters), join(firsts), join(seconds))


def solution(mesh):
    state = P("book", "dp", None)
    return jax.shard_map(
        per_device,
        mesh=mesh,
        in_specs=(P("dp", None), P("dp", "book"), state, state, state),
        out_specs=(state, state, state),
        check_vma=False,
    )
```

time: 631 us -> 294 us (0.47)
  waiting for transfers between devices: 297 us -> 52 us
  blocking collectives: 165 us -> 115 us
  local copies, waits for them, and re-layouts: 40.3 us -> 23.5 us
  between operations: 14.3 us -> 0.86 us
  Pallas kernels: 88.7 us -> 76.9 us
    psum x2 -> x0, waiting for transfers between devices: 238 us -> none  [per_device(): dots = lax.psum(dots, AXES)]
    all_gather x1 -> x0, blocking collectives: 81.4 us -> none  [per_device(): ids = lax.all_gather(code_ids.T, AXES, axis=0)]
    all_to_all x2 -> x6, blocking collectives: 83.7 us -> 115 us  [exchange(): return lax.all_to_all(array, AXES, 0, 0)]
    pallas_call x2, Pallas kernels: 56 us -> 32.7 us  [run_recon(): pl.pallas_call(recon_kernel, grid=(tokens // CHUNK,), in_specs=[by_token(...]
    unnamed x32 -> x11, local copies, waits for them, and re-layouts: 21.9 us -> 6.1 us
    pallas_call x2 -> x4, Pallas kernels: 32.7 us -> 44.3 us  [the longest x2 32.5 us: run_grad(): pl.pallas_call(functools.partial(grad_kernel, shrink), grid=(tokens // CH...]
    all_to_all x2 -> x3, waiting for transfers between devices: 43.1 us -> 35.1 us  [exchange(): return lax.all_to_all(array, AXES, 0, 0)]
    transpose x6 -> x3, local copies, waits for them, and re-layouts: 9.43 us -> 1.84 us  [the longest x1 1.11 us: books_out(): return cut.transpose(2, 0, 3, 1)]
  transfers between devices with their start and end apart: 5 -> 4, of which waited for: 4 -> 4; matrix products, arithmetic and copies ran while one was open for 1% -> 3% of each run, Pallas kernels for 0% -> 0%
where the time goes in v2:
time: 294 us; the launch traced here: 293 us
  blocking collectives  115 us (39%)
  Pallas kernels  76.9 us (26%)
  waiting for transfers between devices  52 us (18%)
  local copies, waits for them, and re-layouts  23.5 us (8%)
  starting transfers between devices  19.6 us (7%)
  other arithmetic  4.99 us (2%)
    all_to_all x6, blocking collectives, exchange(): return lax.all_to_all(array, AXES, 0, 0)  115 us
    all_to_all x3, waiting for transfers between devices, exchange(): return lax.all_to_all(array, AXES, 0, 0)  35.1 us
    pallas_call x2, Pallas kernels, run_recon(): pl.pallas_call(recon_kernel, grid=(tokens // CHUNK,), in_specs=[by_token(...  32.7 us
    pallas_call x2, Pallas kernels, run_grad(): pl.pallas_call(functools.partial(grad_kernel, shrink), grid=(tokens // CH...  32.5 us
    all_to_all x1, waiting for transfers between devices, per_device(): corpus = lax.all_to_all(mine.transpose(1, 2, 0), 'dp', 0, 0)  16.9 us
    all_to_all x3, starting transfers between devices, exchange(): return lax.all_to_all(array, AXES, 0, 0)  15.3 us
    pallas_call x2, Pallas kernels, run_adam(): pl.pallas_call(functools.partial(adam_kernel, grow), grid=(books,), in_sp...  11.7 us
    unnamed x11, local copies, waits for them, and re-layouts  6.1 us
  transfers between devices with their start and end apart: 4, of which 4 were waited for; matrix products, arithmetic and copies ran while one was open for 3% of the time, Pallas kernels for 0%

profile of v2, /device:TPU:0, one launch (start us, length us, event | category | flops | bytes accessed | tf_op | source)
XLA Modules:
  0.0 292.6 jit_solution(6636726546147952212)
XLA Ops:
  0.6 0.7 convert_bitcast_fusion.1
  1.3 0.7 broadcast_in_dim.6
  2.1 7.3 %all-to-all-start = ((s16[32,4,768]{2,1,0:T(4,128)(2,1)}), s16[32,4,768]{2,1,0:T(4,128)(2,1)S(1)}, u32[]{:S(2)}, u32[]{:S(2)}) async-start(s16[32,4,768]{2,1,0:T(4,128)(2,1)} %broadcast_in_dim.6), calls=%async_computation | async-start | bytes 393216 | tf_op jit(solution)/shard_map/all_to_all | solution.py:177
  9.4 2.6 copy.37
  12.0 2.2 dynamic-slice_bitcast_fusion
  14.2 4.9 %all-to-all-done = s16[32,4,768]{2,1,0:T(4,128)(2,1)S(1)} async-done(((s16[32,4,768]{2,1,0:T(4,128)(2,1)}), s16[32,4,768]{2,1,0:T(4,128)(2,1)S(1)}, u32[]{:S(2)}, u32[]{:S(2)}) %all-to-all-start) | async-done | bytes 196640 | tf_op jit(solution)/shard_map/all_to_all | solution.py:177
  19.0 4.3 %all-to-all-start.2 = ((bf16[16,32,768]{2,1,0:T(8,128)(2,1)}), bf16[16,32,768]{2,1,0:T(8,128)(2,1)}, u32[]{:S(2)}, u32[]{:S(2)}) async-start(bf16[16,32,768]{2,1,0:T(8,128)(2,1)} %dynamic-slice_bitcast_fusion), calls=%async_computation.2 | async-start | bytes 1572864 | tf_op jit(solution)/shard_map/all_to_all | solution.py:194
  23.3 0.7 copy.33
  24.1 1.1 copy.34
  25.2 16.9 %all-to-all-done.2 = bf16[16,32,768]{2,1,0:T(8,128)(2,1)} async-done(((bf16[16,32,768]{2,1,0:T(8,128)(2,1)}), bf16[16,32,768]{2,1,0:T(8,128)(2,1)}, u32[]{:S(2)}, u32[]{:S(2)}) %all-to-all-start.2) | async-done | bytes 786464 | tf_op jit(solution)/shard_map/all_to_all | solution.py:194
  42.1 4.4 %all-to-all-start.1 = ((bf16[32,4,32,128]{3,2,1,0:T(8,128)(2,1)}), bf16[32,4,32,128]{3,2,1,0:T(8,128)(2,1)S(1)}, u32[]{:S(2)}, u32[]{:S(2)}) async-start(bf16[32,4,32,128]{3,2,1,0:T(8,128)(2,1)} %copy.34), calls=%async_computation.1 | async-start | bytes 2097152 | tf_op jit(solution)/shard_map/all_to_all | solution.py:177
  46.6 0.1 copy.32
  46.7 0.2 copy.48
  47.0 1.2 copy.47
  48.1 24.6 %all-to-all-done.1 = bf16[32,4,32,128]{3,2,1,0:T(8,128)(2,1)S(1)} async-done(((bf16[32,4,32,128]{3,2,1,0:T(8,128)(2,1)}), bf16[32,4,32,128]{3,2,1,0:T(8,128)(2,1)S(1)}, u32[]{:S(2)}, u32[]{:S(2)}) %all-to-all-start.1) | async-done | bytes 1048608 | tf_op jit(solution)/shard_map/all_to_all | solution.py:177
  72.7 0.7 copy.56
  73.4 0.4 reshape.106
  73.8 0.3 copy.36
  74.0 16.6 %lookup.2 = (f32[32,12288]{1,0:T(8,128)S(1)}, f32[1,12288]{1,0:T(1,128)}) custom-call(s32[8,12288]{1,0:T(8,128)S(1)} %bitcast.64, bf16[8,256,256]{2,1,0:T(8,128)(2,1)S(1)} %bitcast.56, bf16[32,12288]{1,0:T(8,128)(2,1)S(1)} %bitcast.58, bf16[32,12288]{1,0:T(8,128)(2,1)S(1)} %bitcast.59), custom_call_target="tpu_custom_call" | custom-call | flops 12884901888 | bytes 3932160 | tf_op jit(solution)/shard_map/lookup/pallas_call | solution.py:92
  90.7 3.6 %all-to-all-start.3 = ((f32[32,1,384]{2,1,0:T(1,128)}), f32[32,1,384]{2,1,0:T(1,128)S(1)}, u32[]{:S(2)}, u32[]{:S(2)}) async-start(f32[32,1,384]{2,1,0:T(1,128)} %bitcast.13), calls=%async_computation.3 | async-start | bytes 98304 | tf_op jit(solution)/shard_map/all_to_all | solution.py:177
  94.3 1.8 multiply_reduce_fusion
  96.1 5.7 %all-to-all-done.3 = f32[32,1,384]{2,1,0:T(1,128)S(1)} async-done(((f32[32,1,384]{2,1,0:T(1,128)}), f32[32,1,384]{2,1,0:T(1,128)S(1)}, u32[]{:S(2)}, u32[]{:S(2)}) %all-to-all-start.3) | async-done | bytes 49184 | tf_op jit(solution)/shard_map/all_to_all | solution.py:177
  101.9 9.2 %all_to_all.60 = f32[32,1,384]{2,1,0:T(1,128)S(1)} all-to-all(f32[32,1,384]{2,1,0:T(1,128)S(1)} %broadcast_in_dim.7), channel_id=1, replica_groups=mesh['dp'=16,'book'=2] {'dp','book'}, dimensions={0} | all-to-all | bytes 98304 | tf_op jit(solution)/shard_map/all_to_all | solution.py:177
  111.1 16.3 %scatter.2 = f32[8,256,256]{2,1,0:T(8,128)S(1)} custom-call(s32[8,12288]{1,0:T(8,128)S(1)} %bitcast.65, f32[32,12288]{1,0:T(8,128)S(1)} %get-tuple-element.11.resid_ref, bf16[32,12288]{1,0:T(8,128)(2,1)S(1)} %bitcast.60, f32[1,12288]{1,0:T(1,128)S(1)} %bitcast.69), custom_call_target="tpu_custom_call" | custom-call | flops 12884901888 | bytes 3932160 | tf_op jit(solution)/shard_map/scatter/pallas_call | solution.py:114
  127.4 0.2 convert_element_type.41
  127.6 0.9 copy.55
  128.4 0.5 reshape.112
  128.9 0.4 copy.41
  129.3 28.0 %all_to_all.61 = f16[32,4,32,128]{3,2,1,0:T(8,128)(2,1)S(1)} all-to-all(f16[32,4,32,128]{3,2,1,0:T(8,128)(2,1)S(1)} %bitcast.79), channel_id=1, replica_groups=mesh['dp'=16,'book'=2] {'dp','book'}, dimensions={0} | all-to-all | bytes 2097152 | tf_op jit(solution)/shard_map/all_to_all | solution.py:177
  157.2 1.6 convert_element_type.44.grad_ref
  158.8 5.8 %adam.2 = (f32[4,128,1024]{2,1,0:T(8,128)S(1)}, f32[4,128,1024]{2,1,0:T(8,128)S(1)}, f32[4,128,1024]{2,1,0:T(8,128)}, bf16[32,4,32,128]{3,2,1,0:T(8,128)(2,1)S(1)}) custom-call(f32[32,4,32,128]{3,2,1,0:T(8,128)} %convert_element_type.44.grad_ref, f32[4,128,1024]{2,1,0:T(8,128)} %master_ref.1, f32[4,128,1024]{2,1,0:T(8,128)} %first_ref.1, ...), custom_call_target="tpu_custom_call" | custom-call | flops 10485760 | bytes 14680064 | tf_op jit(solution)/shard_map/adam/pallas_call | solution.py:138
  164.7 29.6 %all_to_all.62 = bf16[32,4,32,128]{3,2,1,0:T(8,128)(2,1)S(1)} all-to-all(bf16[32,4,32,128]{3,2,1,0:T(8,128)(2,1)S(1)} %get-tuple-element.13), channel_id=1, replica_groups=mesh['dp'=16,'book'=2] {'dp','book'}, dimensions={0} | all-to-all | bytes 2097152 | tf_op jit(solution)/shard_map/all_to_all | solution.py:177
  194.2 1.6 copy.54
  195.9 2.2 reshape.115
  198.1 1.5 copy.43
  199.6 16.0 %lookup.3 = (f32[32,12288]{1,0:T(8,128)S(1)}, f32[1,12288]{1,0:T(1,128)S(1)}) custom-call(s32[8,12288]{1,0:T(8,128)S(1)} %bitcast.66, bf16[8,256,256]{2,1,0:T(8,128)(2,1)S(1)} %bitcast.57, bf16[32,12288]{1,0:T(8,128)(2,1)S(1)} %bitcast.61, bf16[32,12288]{1,0:T(8,128)(2,1)S(1)} %bitcast.62), custom_call_target="tpu_custom_call" | custom-call | flops 12884901888 | bytes 3932160 | tf_op jit(solution)/shard_map/lookup/pallas_call | solution.py:92
  215.6 1.1 copy-done.1
  216.7 10.9 %all_to_all.63 = f32[32,1,384]{2,1,0:T(1,128)S(1)} all-to-all(f32[32,1,384]{2,1,0:T(1,128)S(1)} %bitcast.70), channel_id=1, replica_groups=mesh['dp'=16,'book'=2] {'dp','book'}, dimensions={0} | all-to-all | bytes 98304 | tf_op jit(solution)/shard_map/all_to_all | solution.py:177
  227.8 9.2 %all_to_all.64 = f32[32,1,384]{2,1,0:T(1,128)S(1)} all-to-all(f32[32,1,384]{2,1,0:T(1,128)S(1)} %broadcast_in_dim.8), channel_id=1, replica_groups=mesh['dp'=16,'book'=2] {'dp','book'}, dimensions={0} | all-to-all | bytes 98304 | tf_op jit(solution)/shard_map/all_to_all | solution.py:177
  236.9 1.4 copy-done.2
  238.4 16.2 %scatter.3 = f32[8,256,256]{2,1,0:T(8,128)S(1)} custom-call(s32[8,12288]{1,0:T(8,128)S(1)} %bitcast.67, f32[32,12288]{1,0:T(8,128)S(1)} %copy-done.2, bf16[32,12288]{1,0:T(8,128)(2,1)S(1)} %bitcast.63, f32[1,12288]{1,0:T(1,128)S(1)} %bitcast.68), custom_call_target="tpu_custom_call" | custom-call | flops 12884901888 | bytes 3932160 | tf_op jit(solution)/shard_map/scatter/pallas_call | solution.py:114
  254.6 0.2 convert_element_type.45
  254.8 1.8 copy.53
  256.6 1.5 reshape.118
  258.1 0.4 copy.46
  258.5 28.0 %all_to_all.65 = f16[32,4,32,128]{3,2,1,0:T(8,128)(2,1)S(1)} all-to-all(f16[32,4,32,128]{3,2,1,0:T(8,128)(2,1)S(1)} %bitcast.85), channel_id=1, replica_groups=mesh['dp'=16,'book'=2] {'dp','book'}, dimensions={0} | all-to-all | bytes 2097152 | tf_op jit(solution)/shard_map/all_to_all | solution.py:177
  286.4 0.3 convert_element_type.48.grad_ref
  286.7 5.9 %adam.3 = (f32[4,128,1024]{2,1,0:T(8,128)}, f32[4,128,1024]{2,1,0:T(8,128)}, f32[4,128,1024]{2,1,0:T(8,128)}) custom-call(f32[32,4,32,128]{3,2,1,0:T(8,128)S(1)} %convert_element_type.48.grad_ref, f32[4,128,1024]{2,1,0:T(8,128)S(1)} %get-tuple-element.16.master_ref, f32[4,128,1024]{2,1,0:T(8,128)} %copy-done, f32[4,128,1024]{2,1,0:T(8,128)} %get-tuple-element.18.second_ref), custom_call_target="tpu_custom_call" | custom-call | flops 10485760 | bytes 14680064 | tf_op jit(solution)/shard_map/adam/pallas_call | solution.py:138
  (16 shorter events, 0.4 us)
Async XLA Ops:
  2.1 17.0 %all-to-all-start = ((s16[32,4,768]{2,1,0:T(4,128)(2,1)}), s16[32,4,768]{2,1,0:T(4,128)(2,1)S(1)}, u32[]{:S(2)}, u32[]{:S(2)}) async-start(s16[32,4,768]{2,1,0:T(4,128)(2,1)} %broadcast_in_dim.6), calls=%async_computation | async-start | bytes 393216 | tf_op jit(solution)/shard_map/all_to_all | solution.py:177
  12.0 11.4 %copy-start.3 = (f32[4,128,1024]{2,1,0:T(8,128)S(1)}, f32[4,128,1024]{2,1,0:T(8,128)}, u32[]{:S(2)}) copy-start(f32[4,128,1024]{2,1,0:T(8,128)} %master_ref.1) | copy-start | bytes 6291460
  19.0 23.0 %all-to-all-start.2 = ((bf16[16,32,768]{2,1,0:T(8,128)(2,1)}), bf16[16,32,768]{2,1,0:T(8,128)(2,1)}, u32[]{:S(2)}, u32[]{:S(2)}) async-start(bf16[16,32,768]{2,1,0:T(8,128)(2,1)} %dynamic-slice_bitcast_fusion), calls=%async_computation.2 | async-start | bytes 1572864 | tf_op jit(solution)/shard_map/all_to_all | solution.py:194
  42.1 30.7 %all-to-all-start.1 = ((bf16[32,4,32,128]{3,2,1,0:T(8,128)(2,1)}), bf16[32,4,32,128]{3,2,1,0:T(8,128)(2,1)S(1)}, u32[]{:S(2)}, u32[]{:S(2)}) async-start(bf16[32,4,32,128]{3,2,1,0:T(8,128)(2,1)} %copy.34), calls=%async_computation.1 | async-start | bytes 2097152 | tf_op jit(solution)/shard_map/all_to_all | solution.py:177
  90.7 11.1 %all-to-all-start.3 = ((f32[32,1,384]{2,1,0:T(1,128)}), f32[32,1,384]{2,1,0:T(1,128)S(1)}, u32[]{:S(2)}, u32[]{:S(2)}) async-start(f32[32,1,384]{2,1,0:T(1,128)} %bitcast.13), calls=%async_computation.3 | async-start | bytes 98304 | tf_op jit(solution)/shard_map/all_to_all | solution.py:177
  164.7 31.2 %copy-start = (f32[4,128,1024]{2,1,0:T(8,128)}, f32[4,128,1024]{2,1,0:T(8,128)S(1)}, u32[]{:S(2)}) copy-start(f32[4,128,1024]{2,1,0:T(8,128)S(1)} %get-tuple-element.17.first_ref) | copy-start | bytes 6291460
  215.6 1.1 copy-start.1
  236.9 1.4 copy-start.2

commit v3 on v2

--- a/solution.py
+++ b/solution.py
@@ -72,7 +72,8 @@
 
 def adam_kernel(grow, grad_ref, master_ref, first_ref, second_ref, *outs):
     width, shard = master_ref.shape[2], master_ref.shape[1]
-    sent = grad_ref[...].astype(jnp.float32).reshape(width, shard) * grow
+    sent = grad_ref[...].reshape(width, shard)
+    sent = decode(sent) if sent.dtype == jnp.int16 else sent * grow
     grad = sent.T
     first = 0.9 * first_ref[0] + 0.1 * grad
     second = 0.99 * second_ref[0] + 0.01 * grad * grad
@@ -149,6 +150,242 @@
     )(grad, master, first, second)
 
 
+CODE_GAIN = 900.0
+CODE_UNIT = 256.0
+
+
+def encode(grad):
+    level = jnp.log2(1.0 + jnp.abs(grad) * CODE_UNIT) * CODE_GAIN + 0.5
+    level = level.astype(jnp.int32)
+    return jnp.where(grad < 0.0, -level, level).astype(jnp.int16)
+
+
+def decode(code):
+    level = code.astype(jnp.int32).astype(jnp.float32)
+    size = (jnp.exp2(jnp.abs(level) * (1.0 / CODE_GAIN)) - 1.0) * (1.0 / CODE_UNIT)
+    return jnp.where(level < 0.0, -size, size)
+
+
+def step_kernel(
+    ids_ref, out_books_ref, corpus_ref, squares_ref, got_ref,
+    books_in, table, resid, dots_out, dots_in, coef_out, coef_in, acc, grads_out, grads_in,
+    book_send, book_recv, dots_send, dots_recv, coef_send, coef_recv, grad_send, grad_recv,
+):
+    dp, book = lax.axis_size("dp"), lax.axis_size("book")
+    devices = dp * book
+    my_d, my_b = lax.axis_index("dp"), lax.axis_index("book")
+    me = my_d * book + my_b
+    local_books, cols, shard = books_in.shape[1:]
+    tokens = ids_ref.shape[1]
+    piece = tokens // devices
+    chunk = 4 * piece
+    chunks = tokens // chunk
+    per_low = LOW // shard
+    groups = dp // per_low
+
+    def others(body):
+        def one(i, carry):
+            other = lax.rem(me + i, devices)
+            body(other)
+            return carry
+
+        lax.fori_loop(1, devices, one, 0)
+
+    def copy_to(source, target, send, recv, d, b):
+        return pltpu.make_async_remote_copy(
+            src_ref=source, dst_ref=target, send_sem=send, recv_sem=recv,
+            device_id=(d, b), device_id_type=pl.DeviceIdType.MESH,
+        )
+
+    barrier = pltpu.get_barrier_semaphore()
+
+    def greet(other):
+        pl.semaphore_signal(
+            barrier, inc=1, device_id=(other // book, lax.rem(other, book)),
+            device_id_type=pl.DeviceIdType.MESH,
+        )
+
+    others(greet)
+    pl.semaphore_wait(barrier, devices - 1)
+
+    def book_copy(slot, other, origin):
+        return copy_to(
+            out_books_ref.at[other, slot], books_in.at[origin, slot],
+            book_send.at[slot, other], book_recv.at[slot, origin], other // book, lax.rem(other, book),
+        )
+
+    def send_slot(slot, carry):
+        others(lambda other: book_copy(slot, other, me).start())
+        return carry
+
+    lax.fori_loop(0, local_books, send_slot, 0)
+    books_in[me] = out_books_ref[me]
+    resid[...] = corpus_ref[...].astype(jnp.float32)
+
+    def look_up(slot, carry):
+        others(lambda other: book_copy(slot, other, other).wait_recv())
+        for b in range(book):
+            for d in range(dp):
+                g, q = d // per_low, d % per_low
+                table[b, g * cols : (g + 1) * cols, q * shard : (q + 1) * shard] = books_in[d * book + b, slot]
+
+        def one(c, inner):
+            span = pl.ds(pl.multiple_of(c * chunk, chunk), chunk)
+            total = resid[:, span]
+            for b in range(book):
+                ids = ids_ref[pl.ds(b * local_books + slot, 1), span]
+                high = ids // LOW
+                picked = jnp.dot(
+                    table[b], one_hot_of(ids - high * LOW, chunk), preferred_element_type=jnp.float32
+                )
+                for g in range(groups):
+                    total = total - jnp.where(high == g, picked[g * cols : (g + 1) * cols, :], 0.0)
+            resid[:, span] = total
+            return inner
+
+        lax.fori_loop(0, chunks, one, 0)
+        return carry
+
+    lax.fori_loop(0, local_books, look_up, 0)
+
+    def dot_chunk(c, carry):
+        span = pl.ds(pl.multiple_of(c * chunk, chunk), chunk)
+        dots = jnp.sum(resid[:, span] * corpus_ref[:, span].astype(jnp.float32), axis=0, keepdims=True)
+        for i in range(4):
+            dots_out[c * 4 + i] = dots[:, i * piece : (i + 1) * piece]
+        return carry
+
+    lax.fori_loop(0, chunks, dot_chunk, 0)
+
+    def dot_copy(other, origin):
+        return copy_to(
+            dots_out.at[other], dots_in.at[origin], dots_send.at[other], dots_recv.at[origin],
+            other // book, lax.rem(other, book),
+        )
+
+    others(lambda other: dot_copy(other, me).start())
+    dots_in[me] = dots_out[me]
+    others(lambda other: dot_copy(other, other).wait_recv())
+    coef = 3.0 * jnp.sum(dots_in[...], axis=0) / (squares_ref[...] + 1e-06)
+    coef_out[...] = coef
+
+    def coef_copy(other, origin):
+        return copy_to(
+            coef_out, coef_in.at[origin], coef_send.at[other], coef_recv.at[origin],
+            other // book, lax.rem(other, book),
+        )
+
+    others(lambda other: coef_copy(other, me).start())
+    coef_in[me] = coef
+    others(lambda other: coef_copy(other, other).wait_recv())
+
+    def pull_chunk(c, carry):
+        span = pl.ds(pl.multiple_of(c * chunk, chunk), chunk)
+        scale = jnp.concatenate([coef_in[c * 4 + i] for i in range(4)], axis=1)
+        pull = resid[:, span] + scale * corpus_ref[:, span].astype(jnp.float32)
+        resid[:, span] = pull.astype(jnp.bfloat16).astype(jnp.float32)
+        return carry
+
+    lax.fori_loop(0, chunks, pull_chunk, 0)
+
+    def grad_copy(slot, d, b, origin):
+        return copy_to(
+            grads_out.at[slot, d * book + b], grads_in.at[origin, slot],
+            grad_send.at[slot, d * book + b], grad_recv.at[slot, origin], d, b,
+        )
+
+    def scatter(turn, carry):
+        slot, b = turn // book, lax.rem(turn, book)
+        row = pl.ds(b * local_books + slot, 1)
+        acc[...] = jnp.zeros_like(acc)
+
+        def one(c, inner):
+            span = pl.ds(pl.multiple_of(c * chunk, chunk), chunk)
+            ids = ids_ref[row, span]
+            high = ids // LOW
+            pull = resid[:, span]
+            spread = jnp.concatenate(
+                [jnp.where(high == g, pull, 0.0).astype(jnp.bfloat16) for g in range(groups)], axis=0
+            )
+            acc[...] += lax.dot_general(
+                spread, one_hot_of(ids - high * LOW, chunk), (((1,), (1,)), ((), ())),
+                preferred_element_type=jnp.float32,
+            )
+            return inner
+
+        lax.fori_loop(0, chunks, one, 0)
+        for d in range(dp):
+            g, q = d // per_low, d % per_low
+            tile = acc[g * cols : (g + 1) * cols, q * shard : (q + 1) * shard]
+            grads_out[slot, d * book + b] = encode(-2.0 * tile)
+
+        def send(i, inner):
+            d = lax.rem(my_d + i, dp)
+
+            @pl.when(d * book + b != me)
+            def _():
+                grad_copy(slot, d, b, me).start()
+
+            return inner
+
+        lax.fori_loop(0, dp, send, 0)
+        return carry
+
+    lax.fori_loop(0, local_books * book, scatter, 0)
+
+    def finish(slot, carry):
+        grads_in[me, slot] = grads_out[slot, me]
+
+        def one(other):
+            grad_copy(slot, other // book, lax.rem(other, book), other).wait()
+            book_copy(slot, other, me).wait_send()
+
+        others(one)
+        return carry
+
+    lax.fori_loop(0, local_books, finish, 0)
+    others(lambda other: dot_copy(other, me).wait_send())
+    others(lambda other: coef_copy(other, me).wait_send())
+    got_ref[...] = grads_in[...]
+
+
+def run_step(ids, outgoing, corpus, squares):
+    devices, local_books, cols, shard = outgoing.shape
+    books, tokens = ids.shape
+    dp = lax.axis_size("dp")
+    piece = tokens // devices
+    dma = lambda *shape: pltpu.SemaphoreType.DMA(shape)
+    moved = (devices, local_books, cols, shard)
+    return pl.pallas_call(
+        step_kernel,
+        in_specs=[pl.BlockSpec(memory_space=pltpu.VMEM)] * 4,
+        out_specs=pl.BlockSpec(memory_space=pltpu.VMEM),
+        out_shape=jax.ShapeDtypeStruct(moved, jnp.int16),
+        scratch_shapes=[
+            pltpu.VMEM(moved, jnp.bfloat16),
+            pltpu.VMEM((lax.axis_size("book"), dp * shard // LOW * cols, LOW), jnp.bfloat16),
+            pltpu.VMEM((cols, tokens), jnp.float32),
+            pltpu.VMEM((devices, 1, piece), jnp.float32),
+            pltpu.VMEM((devices, 1, piece), jnp.float32),
+            pltpu.VMEM((1, piece), jnp.float32),
+            pltpu.VMEM((devices, 1, piece), jnp.float32),
+            pltpu.VMEM((dp * shard // LOW * cols, LOW), jnp.float32),
+            pltpu.VMEM((local_books, devices, cols, shard), jnp.int16),
+            pltpu.VMEM(moved, jnp.int16),
+            dma(local_books, devices), dma(local_books, devices),
+            dma(devices), dma(devices), dma(devices), dma(devices),
+            dma(local_books, devices), dma(local_books, devices),
+        ],
+        cost_estimate=pl.CostEstimate(
+            flops=4 * books * tokens * dp * shard * cols, bytes_accessed=2**23, transcendentals=0
+        ),
+        compiler_params=pltpu.CompilerParams(
+            vmem_limit_bytes=VMEM, collective_id=0, has_side_effects=True
+        ),
+        name="step",
+    )(ids, outgoing, corpus, squares)
+
+
 def per_device(corpus_rows, code_ids, master, first_moment, second_moment):
     local_books, shard, width = master.shape
     local_rows = corpus_rows.shape[0]
@@ -199,6 +436,15 @@
     squares = lax.dynamic_index_in_dim(squares, lax.axis_index("book"), 0, keepdims=False)
 
     outgoing = [books_out(part) for part in masters]
+    fused = cols % 16 == 0 and shard % 128 == 0 and LOW % shard == 0 and (tokens // devices) % 128 == 0
+    if fused:
+        state = (master, first_moment, second_moment)
+        outgoing = outgoing[0]
+        for turn in range(STEPS):
+            codes = run_step(ids[0], outgoing, corpus, squares[None])
+            out = run_adam(codes, *state, 1.0, turn + 1 < STEPS)
+            state, outgoing = tuple(out[:3]), out[-1]
+        return state
     for turn in range(STEPS):
         resid = corpus
         for p in range(parts):

time: 294 us -> 234 us (0.80)
  blocking collectives: 115 us -> 0 us
  Pallas kernels: 76.9 us -> 189 us
  waiting for transfers between devices: 52 us -> 20.4 us
  local copies, waits for them, and re-layouts: 23.5 us -> 7.94 us
  starting transfers between devices: 19.6 us -> 11.6 us
    all_to_all x6 -> x0, blocking collectives: 115 us -> none  [exchange(): return lax.all_to_all(array, AXES, 0, 0)]
    pallas_call x4 -> x2, Pallas kernels: 65.2 us -> 177 us  [run_step(): pl.pallas_call(step_kernel, in_specs=[pl.BlockSpec(memory_space=pltpu.VME...]
    all_to_all x3 -> x1, waiting for transfers between devices: 35.1 us -> 4.86 us  [exchange(): return lax.all_to_all(array, AXES, 0, 0)]
    all_to_all x3 -> x1, starting transfers between devices: 15.3 us -> 7.3 us  [exchange(): return lax.all_to_all(array, AXES, 0, 0)]
    reshape x6 -> x1, local copies, waits for them, and re-layouts: 6.86 us -> 0.11 us  [books_out(): cut = part.astype(jnp.bfloat16).reshape(part_books, shard, devices, cols)]
    transpose x5 -> x0, local copies, waits for them, and re-layouts: 3.57 us -> none  [the longest x2 1.73 us: per_device(): table = table.reshape(books, cols, groups, LOW).transpose(0, 2, 1, 3)]
    unnamed x11 -> x7, local copies, waits for them, and re-layouts: 6.1 us -> 3.56 us
  transfers between devices with their start and end apart: 4 -> 2, of which waited for: 4 -> 2; matrix products, arithmetic and copies ran while one was open for 3% -> 3% of each run, Pallas kernels for 0% -> 0%
where the time goes in v3:
time: 234 us; the launch traced here: 232 us
  Pallas kernels  189 us (81%)
  waiting for transfers between devices  20.4 us (9%)
  starting transfers between devices  11.6 us (5%)
  local copies, waits for them, and re-layouts  7.94 us (3%)
  other arithmetic  2.6 us (1%)
    pallas_call x2, Pallas kernels, run_step(): pl.pallas_call(step_kernel, in_specs=[pl.BlockSpec(memory_space=pltpu.VME...  177 us
    all_to_all x1, waiting for transfers between devices, per_device(): corpus = lax.all_to_all(mine.transpose(1, 2, 0), 'dp', 0, 0)  15.5 us
    pallas_call x2, Pallas kernels, run_adam(): pl.pallas_call(functools.partial(adam_kernel, grow), grid=(books,), in_sp...  11.6 us
    all_to_all x1, starting transfers between devices, exchange(): return lax.all_to_all(array, AXES, 0, 0)  7.3 us
    all_to_all x1, waiting for transfers between devices, exchange(): return lax.all_to_all(array, AXES, 0, 0)  4.86 us
  transfers between devices with their start and end apart: 2, of which 2 were waited for; matrix products, arithmetic and copies ran while one was open for 3% of the time, Pallas kernels for 0%

profile of v3, /device:TPU:0, one launch (start us, length us, event | category | flops | bytes accessed | tf_op | source)
XLA Modules:
  0.0 232.2 jit_solution(8130622388873824635)
XLA Ops:
  0.6 0.7 convert_bitcast_fusion.1
  1.3 0.7 broadcast_in_dim.2
  2.1 7.3 %all-to-all-start = ((s16[32,4,768]{2,1,0:T(4,128)(2,1)}), s16[32,4,768]{2,1,0:T(4,128)(2,1)S(1)}, u32[]{:S(2)}, u32[]{:S(2)}) async-start(s16[32,4,768]{2,1,0:T(4,128)(2,1)} %broadcast_in_dim.2), calls=%async_computation | async-start | bytes 393216 | tf_op jit(solution)/shard_map/all_to_all | solution.py:414
  9.4 2.6 %copy.16 = bf16[768,1024]{0,1:T(8,128)(2,1)} copy(bf16[768,1024]{1,0:T(8,128)(2,1)} %param.5) | data formatting | bytes 3145728 | tf_op args[0]
  12.0 0.0 copy-start.1
  12.0 2.2 dynamic-slice_bitcast_fusion
  14.2 4.9 %all-to-all-done = s16[32,4,768]{2,1,0:T(4,128)(2,1)S(1)} async-done(((s16[32,4,768]{2,1,0:T(4,128)(2,1)}), s16[32,4,768]{2,1,0:T(4,128)(2,1)S(1)}, u32[]{:S(2)}, u32[]{:S(2)}) %all-to-all-start) | async-done | bytes 196640 | tf_op jit(solution)/shard_map/all_to_all | solution.py:414
  19.0 4.3 %all-to-all-start.1 = ((bf16[16,32,768]{2,1,0:T(8,128)(2,1)}), bf16[16,32,768]{2,1,0:T(8,128)(2,1)}, u32[]{:S(2)}, u32[]{:S(2)}) async-start(bf16[16,32,768]{2,1,0:T(8,128)(2,1)} %dynamic-slice_bitcast_fusion), calls=%async_computation.1 | async-start | bytes 1572864 | tf_op jit(solution)/shard_map/all_to_all | solution.py:431
  23.3 1.8 multiply_reduce_fusion
  25.1 0.0 copy-done.1
  25.1 0.7 copy.14
  25.9 0.1 copy.21
  26.0 0.1 convert_bitcast_fusion
  26.1 0.1 copy.13
  26.3 0.2 copy.19
  26.5 15.5 %all-to-all-done.1 = bf16[16,32,768]{2,1,0:T(8,128)(2,1)} async-done(((bf16[16,32,768]{2,1,0:T(8,128)(2,1)}), bf16[16,32,768]{2,1,0:T(8,128)(2,1)}, u32[]{:S(2)}, u32[]{:S(2)}) %all-to-all-start.1) | async-done | bytes 786464 | tf_op jit(solution)/shard_map/all_to_all | solution.py:431
  42.0 1.2 copy.18
  43.2 88.4 %step.2.grad_ref = s16[32,4,32,128]{3,2,1,0:T(8,128)(2,1)S(1)} custom-call(s32[8,12288]{1,0:T(8,128)S(1)} %bitcast.24, bf16[32,4,32,128]{3,2,1,0:T(8,128)(2,1)S(1)} %bitcast.21, bf16[32,12288]{1,0:T(8,128)(2,1)S(1)} %bitcast.22, f32[1,384]{1,0:T(1,128)S(1)} %constant_dynamic-slice_fusion.squares_ref), custom_call_target="tpu_custom_call" | custom-call | flops 25769803776 | bytes 8388608 | tf_op jit(solution)/shard_map/step/pallas_call | solution.py:359
  131.7 6.1 %adam.2 = (f32[4,128,1024]{2,1,0:T(8,128)S(1)}, f32[4,128,1024]{2,1,0:T(8,128)}, f32[4,128,1024]{2,1,0:T(8,128)}, bf16[32,4,32,128]{3,2,1,0:T(8,128)(2,1)S(1)}) custom-call(s16[32,4,32,128]{3,2,1,0:T(8,128)(2,1)S(1)} %step.2.grad_ref, f32[4,128,1024]{2,1,0:T(8,128)} %master_ref.1, f32[4,128,1024]{2,1,0:T(8,128)} %first_ref.1, f32[4,128,1024]{2,1,0:T(8,128)} %second_ref.1), custom_call_target="tpu_custom_call" | custom-call | flops 10485760 | bytes 14680064 | tf_op jit(solution)/shard_map/adam/pallas_call | solution.py:139
  137.8 0.0 copy-start
  137.8 88.9 %step.3.grad_ref = s16[32,4,32,128]{3,2,1,0:T(8,128)(2,1)S(1)} custom-call(s32[8,12288]{1,0:T(8,128)S(1)} %bitcast.25, bf16[32,4,32,128]{3,2,1,0:T(8,128)(2,1)S(1)} %get-tuple-element.7.out_books_ref, bf16[32,12288]{1,0:T(8,128)(2,1)S(1)} %bitcast.23, f32[1,384]{1,0:T(1,128)S(1)} %constant_dynamic-slice_fusion.squares_ref), custom_call_target="tpu_custom_call" | custom-call | flops 25769803776 | bytes 8388608 | tf_op jit(solution)/shard_map/step/pallas_call | solution.py:359
  226.6 0.0 copy-done
  226.7 5.5 %adam.3 = (f32[4,128,1024]{2,1,0:T(8,128)}, f32[4,128,1024]{2,1,0:T(8,128)}, f32[4,128,1024]{2,1,0:T(8,128)}) custom-call(s16[32,4,32,128]{3,2,1,0:T(8,128)(2,1)S(1)} %step.3.grad_ref, f32[4,128,1024]{2,1,0:T(8,128)S(1)} %get-tuple-element.8.master_ref, f32[4,128,1024]{2,1,0:T(8,128)S(1)} %copy-done, f32[4,128,1024]{2,1,0:T(8,128)} %get-tuple-element.10.second_ref), custom_call_target="tpu_custom_call" | custom-call | flops 10485760 | bytes 14680064 | tf_op jit(solution)/shard_map/adam/pallas_call | solution.py:139
  (2 shorter events, 0.0 us)
Async XLA Ops:
  2.1 17.0 %all-to-all-start = ((s16[32,4,768]{2,1,0:T(4,128)(2,1)}), s16[32,4,768]{2,1,0:T(4,128)(2,1)S(1)}, u32[]{:S(2)}, u32[]{:S(2)}) async-start(s16[32,4,768]{2,1,0:T(4,128)(2,1)} %broadcast_in_dim.2), calls=%async_computation | async-start | bytes 393216 | tf_op jit(solution)/shard_map/all_to_all | solution.py:414
  12.0 13.2 %copy-start.1 = (f32[4,128,1024]{2,1,0:T(8,128)S(1)}, f32[4,128,1024]{2,1,0:T(8,128)}, u32[]{:S(2)}) copy-start(f32[4,128,1024]{2,1,0:T(8,128)} %master_ref.1) | copy-start | bytes 6291460
  19.0 23.0 %all-to-all-start.1 = ((bf16[16,32,768]{2,1,0:T(8,128)(2,1)}), bf16[16,32,768]{2,1,0:T(8,128)(2,1)}, u32[]{:S(2)}, u32[]{:S(2)}) async-start(bf16[16,32,768]{2,1,0:T(8,128)(2,1)} %dynamic-slice_bitcast_fusion), calls=%async_computation.1 | async-start | bytes 1572864 | tf_op jit(solution)/shard_map/all_to_all | solution.py:431
  137.8 88.9 %copy-start = (f32[4,128,1024]{2,1,0:T(8,128)S(1)}, f32[4,128,1024]{2,1,0:T(8,128)}, u32[]{:S(2)}) copy-start(f32[4,128,1024]{2,1,0:T(8,128)} %get-tuple-element.9.first_ref) | copy-start | bytes 6291460
